TPU v7x, 256 devices: a whole 4x4x8 slice. The times are simulated.
256 devices in a mesh: wide: 16 (over y_lo, x, core), narrow: 16 (over z, y_hi).
Axes of the slice: x: 4, y: 4 (y_hi: 2, y_lo: 2; y = y_hi * 2 + y_lo), z: 8, core: 2. Of those that a mesh axis runs over, the one named last changes fastest.
Arguments:
- batch_index: int32 [1024], P('narrow'), may hold values from 0 to 255
- train_features: float32 [4096, 1024], P('narrow'), may hold values from -6 to 6
- train_labels: float32 [4096, 1000], P('narrow'), may hold values from -12 to 12
- centers: float32 [65536, 1024], P(('wide', 'narrow')), may hold values from -6 to 6
- weights: float32 [65536, 1000], P(('wide', 'narrow')), may hold values from -6 to 6
Outputs:
- new_weights: float32 [65536, 1000], P(('wide', 'narrow'))
- residual: float32 [1024, 1000], P('narrow')
Inputs may be any that keep to these rules, and one draw needn't show every extreme that they name: `batch_index`: entry i names a row of the training shard held by narrow index i // 64.
All inputs are finite; a program needn't handle non-finite values.
Results may differ from a plain program's by a relative error of at most 0.0001.
Values sent between devices are 32-bit elements; how exact they have to be, the bound alone decides.
No kernel may reach another device: no remote copies, remote signals or barrier semaphores. Data moves between devices by JAX's collectives and lax.ppermute only.
A program may use at most 64 MiB of HBM per device.

v0:
```python
import math
import jax
import jax.numpy as jnp
from jax import lax
from jax.sharding import Mesh
from jax.sharding import PartitionSpec as P

NARROW = ("narrow_0", "narrow_1")
WIDE_NARROW = ("wide", "narrow_0", "narrow_1")
step_size = 1.0


def gather_axes(array, axes, dim):
    for axis in reversed(axes):
        array = lax.all_gather(array, axis, axis=dim, tiled=True)
    return array


def per_device(batch_index, train_features, train_labels, centers, weights):
    block = batch_index.shape[0]
    rows = jnp.take(train_features, batch_index, axis=0)
    targets = jnp.take(train_labels, batch_index, axis=0)
    features = centers.shape[1]
    center_sq = jnp.sum(centers * centers, axis=1)
    count = centers.shape[0] * lax.axis_size("wide") * lax.axis_size(NARROW)
    scale = 1.0 / math.sqrt(count)
    piece = gather_axes(rows, NARROW, 0)
    inner = jnp.dot(
        piece, centers.T, precision=lax.Precision.HIGHEST, preferred_element_type=jnp.float32
    )
    piece_sq = jnp.sum(piece * piece, axis=1)
    kernel = jnp.exp(
        (2.0 * features - piece_sq[:, None] - center_sq[None, :] + 2.0 * inner) / 128.0
    )
    batch = kernel.shape[0]
    partial_value = jnp.dot(
        kernel, weights, precision=lax.Precision.HIGHEST, preferred_element_type=jnp.float32
    )
    owner = jnp.where(lax.axis_index("wide") == 0, 1.0, 0.0).astype(jnp.float32)
    placed = lax.dynamic_update_slice_in_dim(
        jnp.zeros((batch, targets.shape[1]), jnp.float32),
        targets * owner,
        lax.axis_index(NARROW) * block,
        0,
    )
    resid_all = lax.psum(partial_value * scale - placed, WIDE_NARROW)
    residual = lax.dynamic_slice_in_dim(resid_all, lax.axis_index(NARROW) * block, block, 0)
    delta = lax.dot_general(
        kernel,
        resid_all,
        (((0,), (0,)), ((), ())),
        precision=lax.Precision.HIGHEST,
        preferred_element_type=jnp.float32,
    )
    new_weights = weights - step_size / batch * delta
    return (new_weights, residual)


def solution(mesh):
    split = Mesh(mesh.devices.reshape(mesh.shape["wide"], 8, 2), ("wide", "narrow_0", "narrow_1"))
    placed = (
        P(NARROW),
        P(NARROW, None),
        P(NARROW, None),
        P(WIDE_NARROW, None),
        P(WIDE_NARROW, None),
    )
    return jax.shard_map(
        per_device,
        mesh=split,
        in_specs=placed,
        out_specs=(P(WIDE_NARROW, None), P(NARROW, None)),
        check_vma=False,
    )
```

profile of v0, /device:TPU:2, one launch (start us, length us, event | category | flops | bytes accessed | tf_op | source)
XLA Modules:
  0.0 375.1 jit_solution(9159140242311068464)
XLA Ops:
  7.2 0.0 copy-start
  7.2 0.0 copy-start.6
  7.2 0.0 all-gather.2.cloned.1.call-start
  7.2 0.8 compare_select_fusion
  8.0 0.7 compare_and_fusion
  8.7 0.0 copy-done
  8.7 0.7 gather_fusion
  9.4 0.1 broadcast_select_fusion
  9.5 10.3 %all_gather.6 = f32[128,1024]{1,0:T(8,128)} all-gather(f32[64,1024]{1,0:T(8,128)S(1)} %broadcast_select_fusion), channel_id=1, replica_groups=mesh['wide'=16,'narrow_0'=8,'narrow_1'=2] {'narrow_1'}, dimensions={0}, use_global_device_ids=true | all-gather | bytes 786432 | tf_op jit(solution)/shard_map/all_gather | solution.py:15
  19.8 0.0 all-gather.2.cloned.1.call-update
  19.8 0.0 all-reduce.2.cloned.1.call-start
  19.9 0.0 copy-done.6
  19.9 0.3 copy.7
  20.3 0.0 copy-start.3
  20.3 0.7 gather_fusion.1
  21.0 0.2 copy.8
  21.2 2.5 broadcast_in_dim.30
  23.7 3.5 dynamic_update_slice.3
  27.1 0.0 copy-done.3
  27.1 0.1 multiply_reduce_fusion.1
  27.3 50.5 %all-gather.2.cloned.1.call-done = f32[1024,1024]{1,0:T(8,128)} async-done(((f32[128,1024]{1,0:T(8,128)}), f32[1024,1024]{1,0:T(8,128)}) %all-gather.2.cloned.1.call-update) | async-done | bytes 4194320 | tf_op jit(solution)/shard_map/all_gather | solution.py:15
  77.8 0.0 copy-start.1
  77.8 2.7 multiply_reduce_fusion
  80.5 0.0 copy-start.2
  80.5 0.0 copy-start.4
  80.5 0.7 copy-done.1
  81.2 3.5 fusion.2
  84.8 0.0 copy-done.2
  84.8 0.0 copy-done.4
  84.8 5.3 %multiply_subtract_fusion = f32[1024,1000]{0,1:T(8,128)} fusion(f32[1024,1000]{0,1:T(8,128)S(1)} %copy-done.2, f32[1024,256]{1,0:T(8,128)S(1)} %fusion.2, f32[256,1000]{0,1:T(8,128)S(1)} %copy-done.4), kind=kOutput, calls=%fused_computation.3 | convolution fusion | flops 3147776000 | bytes 10264576 | tf_op jit(solution)/shard_map/dot_general | solution.py:36
  90.1 0.0 copy-start.5
  90.1 0.0 all-reduce.2.cloned.1.call-update
  90.1 267.7 %all-reduce.2.cloned.1.call-done = f32[1024,1000]{0,1:T(8,128)} async-done(((f32[1024,1000]{0,1:T(8,128)}), f32[1024,1000]{0,1:T(8,128)}) %all-reduce.2.cloned.1.call-update) | async-done | bytes 4096016 | tf_op jit(solution)/shard_map/psum | solution.py:46
  357.8 2.0 constant_dynamic-slice_fusion
  359.8 1.9 copy.9
  361.7 0.0 copy-done.5
  361.7 6.5 %fusion.3 = f32[256,1000]{0,1:T(8,128)} fusion(f32[256,1000]{0,1:T(8,128)S(1)} %copy-done.5, f32[1024,256]{1,0:T(8,128)S(1)} %fusion.2, f32[1024,1000]{0,1:T(8,128)} %all-reduce.2.cloned.1.call-done), kind=kOutput, calls=%fused_computation.9 | convolution fusion | flops 3146240000 | bytes 7192576 | tf_op jit(solution)/shard_map/dot_general | solution.py:48
  (3 shorter events, 0.0 us)
Async XLA Ops:
  7.2 1.5 copy-start
  7.2 12.7 %copy-start.6 = (f32[256,1000]{0,1:T(8,128)S(1)}, f32[256,1000]{0,1:T(8,128)}, u32[]{:S(2)}) copy-start(f32[256,1000]{0,1:T(8,128)} %param.7) | copy-start | bytes 3072004
  7.2 70.6 %all-gather.2.cloned.1.call-start = ((), (), s32[]{:S(2)}) async-start(), calls=%async_computation | async-start | bytes 4718592 | tf_op jit(solution)/shard_map/all_gather | solution.py:15
  19.8 337.9 %all-reduce.2.cloned.1.call-start = ((), (), s32[]{:S(2)}) async-start(), calls=%async_computation.1 | async-start | bytes 8192000 | tf_op jit(solution)/shard_map/psum | solution.py:46
  20.3 6.9 %copy-start.3 = (f32[256,1024]{1,0:T(8,128)S(1)}, f32[256,1024]{1,0:T(8,128)}, u32[]{:S(2)}) copy-start(f32[256,1024]{1,0:T(8,128)} %param.8) | copy-start | bytes 3145732
  77.8 3.4 copy-start.1
  80.5 4.3 %copy-start.2 = (f32[1024,1000]{0,1:T(8,128)S(1)}, f32[1024,1000]{0,1:T(8,128)}, u32[]{:S(2)}) copy-start(f32[1024,1000]{0,1:T(8,128)} %dynamic_update_slice.3) | copy-start | bytes 12288004
  80.5 4.3 %copy-start.4 = (f32[256,1000]{0,1:T(8,128)S(1)}, f32[256,1000]{0,1:T(8,128)}, u32[]{:S(2)}) copy-start(f32[256,1000]{0,1:T(8,128)} %param.9) | copy-start | bytes 3072004
  90.1 271.6 %copy-start.5 = (f32[256,1000]{0,1:T(8,128)S(1)}, f32[256,1000]{0,1:T(8,128)}, u32[]{:S(2)}) copy-start(f32[256,1000]{0,1:T(8,128)} %param.9) | copy-start | bytes 3072004
Sparse Core Ops, SparseCore 0:
  20.0 57.7 all-gather.1
  90.2 267.4 all-reduce.1
where the time goes:
time: 375 us
  waiting for transfers between devices  318 us (85%)
  matrix products  15.3 us (4%)
  between operations  14.2 us (4%)
  local copies, waits for them, and re-layouts  12.5 us (3%)
  blocking collectives  10.3 us (3%)
  other arithmetic  4.42 us (1%)
    psum x1, waiting for transfers between devices, per_device(): resid_all = lax.psum(partial_value * scale - placed, WIDE_NARROW)  268 us
    all_gather x1, waiting for transfers between devices, gather_axes(): array = lax.all_gather(array, axis, axis=dim, tiled=True)  50.5 us
    all_gather x1, blocking collectives, gather_axes(): array = lax.all_gather(array, axis, axis=dim, tiled=True)  10.3 us
  transfers between devices with their start and end apart: 2, of which 2 were waited for; matrix products, arithmetic and copies ran while one was open for 2% of the time, Pallas kernels for 0%

commit v1 on v0

--- a/solution.py
+++ b/solution.py
@@ -43,7 +43,8 @@
         lax.axis_index(NARROW) * block,
         0,
     )
-    resid_all = lax.psum(partial_value * scale - placed, WIDE_NARROW)
+    partial = lax.psum(partial_value * scale - placed, "wide")
+    resid_all = lax.psum(partial, ("narrow_0", "narrow_1"))
     residual = lax.dynamic_slice_in_dim(resid_all, lax.axis_index(NARROW) * block, block, 0)
     delta = lax.dot_general(
         kernel,

time: 375 us -> 451 us (1.20)
  waiting for transfers between devices: 318 us -> 394 us
    psum x1 -> x2, waiting for transfers between devices: 268 us -> 344 us  [the longest x1 214 us: per_device(): resid_all = lax.psum(partial, ('narrow_0', 'narrow_1'))]
  transfers between devices with their start and end apart: 2 -> 3, of which waited for: 2 -> 3; matrix products, arithmetic and copies ran while one was open for 2% -> 2% of each run, Pallas kernels for 0% -> 0%
where the time goes in v1:
time: 451 us
  waiting for transfers between devices  394 us (87%)
  matrix products  15.3 us (3%)
  between operations  13.9 us (3%)
  local copies, waits for them, and re-layouts  12.5 us (3%)
  blocking collectives  10.3 us (2%)
    psum x1, waiting for transfers between devices, per_device(): resid_all = lax.psum(partial, ('narrow_0', 'narrow_1'))  214 us
    psum x1, waiting for transfers between devices, per_device(): partial = lax.psum(partial_value * scale - placed, 'wide')  129 us
    all_gather x1, waiting for transfers between devices, gather_axes(): array = lax.all_gather(array, axis, axis=dim, tiled=True)  50.5 us
    all_gather x1, blocking collectives, gather_axes(): array = lax.all_gather(array, axis, axis=dim, tiled=True)  10.3 us
  transfers between devices with their start and end apart: 3, of which 3 were waited for; matrix products, arithmetic and copies ran while one was open for 2% of the time, Pallas kernels for 0%

profile of v1, /device:TPU:2, one launch (start us, length us, event | category | flops | bytes accessed | tf_op | source)
XLA Modules:
  0.0 450.8 jit_solution(16162171724074611347)
XLA Ops:
  7.2 0.0 copy-start
  7.2 0.0 copy-start.6
  7.2 0.0 all-gather.2.cloned.1.call-start
  7.2 0.8 compare_select_fusion
  8.0 0.7 compare_and_fusion
  8.7 0.0 copy-done
  8.7 0.7 gather_fusion
  9.4 0.1 broadcast_select_fusion
  9.5 10.3 %all_gather.6 = f32[128,1024]{1,0:T(8,128)} all-gather(f32[64,1024]{1,0:T(8,128)S(1)} %broadcast_select_fusion), channel_id=1, replica_groups=mesh['wide'=16,'narrow_0'=8,'narrow_1'=2] {'narrow_1'}, dimensions={0}, use_global_device_ids=true | all-gather | bytes 786432 | tf_op jit(solution)/shard_map/all_gather | solution.py:15
  19.8 0.0 all-gather.2.cloned.1.call-update
  19.8 0.0 all-reduce.3.cloned.1.call-start
  19.9 0.0 copy-done.6
  19.9 0.3 copy.7
  20.3 0.0 copy-start.3
  20.3 0.7 gather_fusion.1
  21.0 0.2 copy.8
  21.2 2.5 broadcast_in_dim.30
  23.7 3.5 dynamic_update_slice.3
  27.1 0.0 copy-done.3
  27.1 0.1 multiply_reduce_fusion.1
  27.3 50.5 %all-gather.2.cloned.1.call-done = f32[1024,1024]{1,0:T(8,128)} async-done(((f32[128,1024]{1,0:T(8,128)}), f32[1024,1024]{1,0:T(8,128)}) %all-gather.2.cloned.1.call-update) | async-done | bytes 4194320 | tf_op jit(solution)/shard_map/all_gather | solution.py:15
  77.8 0.0 copy-start.1
  77.8 2.7 multiply_reduce_fusion
  80.5 0.0 copy-start.2
  80.5 0.0 copy-start.4
  80.5 0.7 copy-done.1
  81.2 3.5 fusion.2
  84.8 0.0 copy-done.2
  84.8 0.0 copy-done.4
  84.8 5.3 %multiply_subtract_fusion = f32[1024,1000]{0,1:T(8,128)} fusion(f32[1024,1000]{0,1:T(8,128)S(1)} %copy-done.2, f32[1024,256]{1,0:T(8,128)S(1)} %fusion.2, f32[256,1000]{0,1:T(8,128)S(1)} %copy-done.4), kind=kOutput, calls=%fused_computation.3 | convolution fusion | flops 3147776000 | bytes 10264576 | tf_op jit(solution)/shard_map/dot_general | solution.py:36
  90.1 0.0 copy-start.5
  90.1 0.0 all-reduce.3.cloned.1.call-update
  90.1 0.0 all-reduce.5.cloned.1.call-start
  90.2 129.3 %all-reduce.3.cloned.1.call-done = f32[1024,1000]{0,1:T(8,128)} async-done(((f32[1024,1000]{0,1:T(8,128)}), f32[1024,1000]{0,1:T(8,128)}) %all-reduce.3.cloned.1.call-update) | async-done | bytes 4096016 | tf_op jit(solution)/shard_map/psum | solution.py:46
  219.5 0.0 all-reduce.5.cloned.1.call-update
  219.5 214.3 %all-reduce.5.cloned.1.call-done = f32[1024,1000]{0,1:T(8,128)} async-done(((f32[1024,1000]{0,1:T(8,128)}), f32[1024,1000]{0,1:T(8,128)}) %all-reduce.5.cloned.1.call-update) | async-done | bytes 4096016 | tf_op jit(solution)/shard_map/psum | solution.py:47
  433.8 2.0 constant_dynamic-slice_fusion
  435.8 1.9 copy.9
  437.8 0.0 copy-done.5
  437.8 6.5 %fusion.3 = f32[256,1000]{0,1:T(8,128)} fusion(f32[256,1000]{0,1:T(8,128)S(1)} %copy-done.5, f32[1024,256]{1,0:T(8,128)S(1)} %fusion.2, f32[1024,1000]{0,1:T(8,128)} %all-reduce.5.cloned.1.call-done), kind=kOutput, calls=%fused_computation.9 | convolution fusion | flops 3146240000 | bytes 7192576 | tf_op jit(solution)/shard_map/dot_general | solution.py:49
  (3 shorter events, 0.0 us)
Async XLA Ops:
  7.2 1.5 copy-start
  7.2 12.7 %copy-start.6 = (f32[256,1000]{0,1:T(8,128)S(1)}, f32[256,1000]{0,1:T(8,128)}, u32[]{:S(2)}) copy-start(f32[256,1000]{0,1:T(8,128)} %param.7) | copy-start | bytes 3072004
  7.2 70.6 %all-gather.2.cloned.1.call-start = ((), (), s32[]{:S(2)}) async-start(), calls=%async_computation | async-start | bytes 4718592 | tf_op jit(solution)/shard_map/all_gather | solution.py:15
  19.8 199.6 %all-reduce.3.cloned.1.call-start = ((), (), s32[]{:S(2)}) async-start(), calls=%async_computation.1 | async-start | bytes 8192000 | tf_op jit(solution)/shard_map/psum | solution.py:46
  20.3 6.9 %copy-start.3 = (f32[256,1024]{1,0:T(8,128)S(1)}, f32[256,1024]{1,0:T(8,128)}, u32[]{:S(2)}) copy-start(f32[256,1024]{1,0:T(8,128)} %param.8) | copy-start | bytes 3145732
  77.8 3.4 copy-start.1
  80.5 4.3 copy-start.2
  80.5 4.3 copy-start.4
  90.1 347.7 %copy-start.5 = (f32[256,1000]{0,1:T(8,128)S(1)}, f32[256,1000]{0,1:T(8,128)}, u32[]{:S(2)}) copy-start(f32[256,1000]{0,1:T(8,128)} %param.9) | copy-start | bytes 3072004
  90.1 343.7 %all-reduce.5.cloned.1.call-start = ((), (), s32[]{:S(2)}) async-start(), calls=%async_computation.2 | async-start | bytes 8192000 | tf_op jit(solution)/shard_map/psum | solution.py:47
Sparse Core Ops, SparseCore 0:
  20.0 57.7 all-gather.1
  90.2 129.2 all-reduce.2
  222.2 211.5 all-reduce.4
